TPU v7x, 256 devices: a whole 4x4x8 slice. The times are simulated.
256 devices in a mesh: tile: 16 (over z, core), lev: 4 (over x), tag: 4 (over y).
Axes of the slice: x: 4, y: 4, z: 8, core: 2. Of those that a mesh axis runs over, the one named last changes fastest.
Arguments:
- parent_field: float32 [8, 32, 256, 1024], P('tag', 'lev', 'tile'), may hold values from -6 to 6
- nest_field: float32 [8, 32, 256, 1024], P('tag', 'lev', 'tile'), may hold values from -6 to 6
- parent_mixing: float32 [32, 256, 1024], P('lev', 'tile'), may hold values from 0.05 to 5
- parent_eastward: float32 [256, 1024], P('tile'), may hold values from 0.02 to 0.12
- parent_northward: float32 [256, 1024], P('tile'), may hold values from 0.02 to 0.12
- nest_eastward: float32 [256, 1024], P('tile'), may hold values from 0.02 to 0.12
- nest_northward: float32 [256, 1024], P('tile'), may hold values from 0.02 to 0.12
- strip_tile: int32 [16, 256], replicated, may hold values from 0 to 15, as said below
- strip_block: int32 [16, 256], replicated, may hold values from 0 to 127
- strip_target: int32 [16, 256], replicated, may hold values from 0 to 127
- strip_count: int32 [16], replicated, may hold values from 1 to 256, as said below
Outputs:
- parent_adjoint: float32 [8, 32, 256, 1024], P('tag', 'lev', 'tile')
- nest_adjoint: float32 [8, 32, 256, 1024], P('tag', 'lev', 'tile')
- bulk_adjoint: float32 [32, 256, 1024], P('lev', 'tile', 'tag')
Inputs may be any that keep to these rules, and one draw needn't show every extreme that they name: `strip_tile`: among the first strip_count[j] entries of row j, every parent tile appears at most 16 times; in the row whose count is 256 every parent tile appears exactly 16 times. `strip_count`: exactly one nest tile lists 256 strips; every other lists at most 128.
All inputs are finite; a program needn't handle non-finite values.
Results may differ from a plain program's by a relative error of at most 0.0003.
Values sent between devices are 32-bit elements; how exact they have to be, the bound alone decides.
A program may use at most 64 MiB of HBM per device.

v0:
```python
import jax
import jax.numpy as jnp
from jax import lax
from jax.sharding import PartitionSpec as P

CAP = 16
NSUB = 3
HIGHEST = lax.Precision.HIGHEST


def extended(cells, sides, width):
    for axis, dim in sides:
        count = lax.axis_size(axis)
        ends = count - 1
        head = lax.slice_in_dim(cells, 0, width, axis=dim)
        tail = lax.slice_in_dim(cells, cells.shape[dim] - width, cells.shape[dim], axis=dim)
        cells = jnp.concatenate(
            [
                lax.ppermute(tail, axis, [(i, (i + 1) % count) for i in range(ends)]),
                cells,
                lax.ppermute(head, axis, [((i + 1) % count, i) for i in range(ends)]),
            ],
            axis=dim,
        )
    return cells


def tridiagonal(source, mixing):
    level_count = mixing.shape[0]
    mixing_up = jnp.concatenate([mixing[1:], jnp.zeros_like(mixing[:1])], axis=0)
    diagonal = 1.0 + mixing + mixing_up
    ratio_now = jnp.zeros_like(mixing[0])
    carry_now = jnp.zeros_like(source[:, 0])
    ratios = []
    carries = []
    for lev_index in range(level_count):
        pivot_now = diagonal[lev_index] + mixing[lev_index] * ratio_now
        ratio_now = -mixing_up[lev_index] / pivot_now
        carry_now = (source[:, lev_index] + mixing[lev_index] * carry_now) / pivot_now
        ratios.append(ratio_now)
        carries.append(carry_now)
    value_now = carries[level_count - 1]
    results = [value_now]
    for lev_index in range(level_count - 2, -1, -1):
        value_now = carries[lev_index] - ratios[lev_index] * value_now
        results.append(value_now)
    return jnp.stack(results[::-1], axis=1)


def relax(padded, eastward):
    center = padded[:-1, 1:-1]
    row_above = padded[:-1, :-2]
    row_below = padded[:-1, 2:]
    north_here = padded[-1, 1:-1]
    north_above = padded[-1, :-2]
    zero_column = jnp.zeros_like(center[:, :, :1])
    east_cell = jnp.concatenate([center[:, :, 1:], zero_column], axis=2)
    west_cell = jnp.concatenate([zero_column, center[:, :, :-1]], axis=2)
    west_rate = jnp.concatenate([jnp.zeros_like(eastward[:, :1]), eastward[:, :-1]], axis=1)
    return (
        center
        + north_here * (row_below - center)
        + north_above * (row_above - center)
        + eastward * (east_cell - center)
        + west_rate * (west_cell - center)
    )


def rims(stacked):
    return extended(stacked, (("tile", 1),), 1)


def advance(start, solved, parent_eastward, parent_northward, nest_eastward, nest_northward):
    tag_count, level_count, row_count, col_count = start.shape
    line_count = tag_count * level_count
    nest_now = start.reshape(line_count, row_count, col_count)
    parent_now = solved.reshape(line_count, row_count, col_count)
    for sub_step in range(NSUB):
        nest_stack = jnp.concatenate([nest_now, nest_northward[None]], axis=0)
        if sub_step == 0:
            parent_stack = jnp.concatenate([parent_now, parent_northward[None]], axis=0)
            padded = rims(jnp.concatenate([parent_stack, nest_stack], axis=0))
            parent_now = relax(padded[: line_count + 1], parent_eastward)
            nest_now = relax(padded[line_count + 1 :], nest_eastward)
        else:
            nest_now = relax(rims(nest_stack), nest_eastward)
    full_shape = (tag_count, level_count, row_count, col_count)
    return (parent_now.reshape(full_shape), nest_now.reshape(full_shape))


def deliver(parent_field, strip_tile, strip_block, strip_target, strip_count):
    tag_count, level_count, row_count, col_count = parent_field.shape
    line_count = tag_count * level_count
    block_count = row_count * col_count // 128
    tile_count, slot_total = strip_tile.shape
    own_index = lax.axis_index("tile")
    positions = jnp.arange(slot_total, dtype=jnp.int32)
    is_live = positions[None, :] < strip_count[:, None]
    from_here = jnp.logical_and(is_live, strip_tile == own_index).astype(jnp.int32)
    slot_rank = jnp.cumsum(from_here, axis=1) - 1
    slot_index = jnp.arange(CAP, dtype=jnp.int32)
    select = from_here[:, None, :] * (slot_rank[:, None, :] == slot_index[None, :, None]).astype(
        jnp.int32
    )
    source_block = jnp.sum(select * strip_block[:, None, :], axis=2).reshape(-1)
    filled = jnp.sum(select, axis=2).reshape(-1).astype(jnp.float32)
    blocks = parent_field.reshape(line_count, block_count, 128)
    packed = jnp.take(blocks, source_block, axis=1) * filled[None, :, None]
    received = lax.all_to_all(packed, "tile", split_axis=1, concat_axis=1, tiled=True)
    own_tile = lax.dynamic_index_in_dim(strip_tile, own_index, 0, keepdims=False)
    own_target = lax.dynamic_index_in_dim(strip_target, own_index, 0, keepdims=False)
    own_count = lax.dynamic_index_in_dim(strip_count, own_index, 0, keepdims=False)
    own_live = (positions < own_count).astype(jnp.int32)
    from_source = (own_tile[:, None] == jnp.arange(tile_count, dtype=jnp.int32)[None, :]).astype(
        jnp.int32
    ) * own_live[:, None]
    own_rank = jnp.sum((jnp.cumsum(from_source, axis=0) - 1) * from_source, axis=1)
    arrival = own_tile * CAP + own_rank
    pick_slot = (arrival[:, None] == jnp.arange(tile_count * CAP, dtype=jnp.int32)[None, :]).astype(
        jnp.float32
    )
    pick_slot = pick_slot * own_live[:, None].astype(jnp.float32)
    place_block = (own_target[:, None] == jnp.arange(block_count, dtype=jnp.int32)[None, :]).astype(
        jnp.float32
    )
    routing = jnp.dot(pick_slot.T, place_block, precision=HIGHEST)
    forcing = jnp.einsum("lic,ib->lbc", received, routing, precision=HIGHEST)
    return forcing.reshape(tag_count, level_count, row_count, col_count)


def shards(
    parent_field,
    nest_field,
    parent_mixing,
    parent_eastward,
    parent_northward,
    nest_eastward,
    nest_northward,
    strip_tile,
    strip_block,
    strip_target,
    strip_count,
):
    tag_count = parent_field.shape[0]
    forcing = deliver(parent_field, strip_tile, strip_block, strip_target, strip_count)
    stacked = jnp.concatenate([parent_field, parent_mixing[None]], axis=0)
    columns = lax.all_to_all(stacked, "lev", split_axis=3, concat_axis=1, tiled=True)
    column_result = tridiagonal(columns[:tag_count], columns[tag_count])
    solved = lax.all_to_all(column_result, "lev", split_axis=1, concat_axis=3, tiled=True)
    parent_adjoint, nest_adjoint = advance(
        nest_field + forcing,
        solved,
        parent_eastward,
        parent_northward,
        nest_eastward,
        nest_northward,
    )
    bulk_adjoint = lax.psum_scatter(
        jnp.sum(parent_adjoint, axis=0), "tag", scatter_dimension=2, tiled=True
    )
    return (parent_adjoint, nest_adjoint, bulk_adjoint)


def solution(mesh):
    in_specs = (
        P("tag", "lev", "tile", None),
        P("tag", "lev", "tile", None),
        P("lev", "tile", None),
        P("tile", None),
        P("tile", None),
        P("tile", None),
        P("tile", None),
        P(),
        P(),
        P(),
        P(),
    )
    out_specs = (
        P("tag", "lev", "tile", None),
        P("tag", "lev", "tile", None),
        P("lev", "tile", "tag"),
    )
    return jax.shard_map(shards, mesh=mesh, in_specs=in_specs, out_specs=out_specs, check_vma=False)
```

profile of v0, /device:TPU:2, one launch (start us, length us, event | category | flops | bytes accessed | tf_op | source)
XLA Modules:
  0.0 209.8 jit_solution(3081090923372214536)
XLA Ops:
  7.2 1.5 pad_maximum_fusion.5
  8.7 6.9 %copy.55 = f32[3,8,16,1024]{2,1,0,3:T(8,128)} copy(f32[3,8,16,1024]{3,2,1,0:T(8,128)S(1)} %pad_maximum_fusion.5) | data formatting | bytes 3145728 | tf_op jit(solution)/shard_map/concatenate | solution.py:146
  15.6 8.3 %reshape.176 = f32[4,1,98304]{2,1,0:T(1,128)} reshape(f32[1024,3,8,16]{3,2,1,0:T(8,128)} %bitcast.230) | data formatting | bytes 3145728
  23.9 5.9 %all-to-all-start = ((f32[4,1,98304]{2,1,0:T(1,128)}), f32[4,1,98304]{2,1,0:T(1,128)S(1)}, u32[]{:S(2)}, u32[]{:S(2)}) async-start(f32[4,1,98304]{2,1,0:T(1,128)} %reshape.176), calls=%async_computation | async-start | bytes 3145728 | tf_op jit(solution)/shard_map/all_to_all | solution.py:147
  29.8 1.1 reshape.159
  31.0 0.6 reduce-window.16
  32.0 0.6 select_reduce_fusion
  32.7 1.8 copy.65
  34.7 13.4 %all-to-all-done = f32[4,1,98304]{2,1,0:T(1,128)S(1)} async-done(((f32[4,1,98304]{2,1,0:T(1,128)}), f32[4,1,98304]{2,1,0:T(1,128)S(1)}, u32[]{:S(2)}, u32[]{:S(2)}) %all-to-all-start) | async-done | bytes 1572896 | tf_op jit(solution)/shard_map/all_to_all | solution.py:147
  48.1 1.2 copy-done.1
  49.2 0.5 broadcast.2764
  49.8 6.2 %reduce.4 = f32[4,98304]{1,0:T(4,128)S(1)} reduce(f32[4,1,98304]{2,1,0:T(1,128)} %copy-done.1, f32[]{:T(128)} %broadcast.2764), dimensions={1}, to_apply=%all_to_all.25.reduce_sub_computation | reduce | bytes 3145732 | tf_op jit(solution)/shard_map/all_to_all | solution.py:147
  55.9 8.9 %reshape.177 = f32[1024,3,8,16]{3,2,1,0:T(8,128)} reshape(f32[4,98304]{1,0:T(4,128)S(1)} %reduce.4) | data formatting | bytes 3145728
  64.8 7.8 %copy.69 = f32[3,8,16,4,256]{4,3,2,1,0:T(4,128)S(1)} copy(f32[3,8,16,4,256]{2,1,0,4,3:T(8,128)} %bitcast.231) | data formatting | bytes 3145728 | tf_op jit(solution)/shard_map/all_to_all | solution.py:147
  74.9 1.0 copy.59
  75.9 5.7 %all-to-all-start.1 = ((f32[2,32,16,256]{3,2,0,1:T(8,128)}), f32[2,32,16,256]{3,2,0,1:T(8,128)}, u32[]{:S(2)}, u32[]{:S(2)}) async-start(f32[2,32,16,256]{3,2,0,1:T(8,128)} %copy.59), calls=%async_computation.1 | async-start | bytes 2097152 | tf_op jit(solution)/shard_map/all_to_all | solution.py:149
  81.6 1.0 gather_fusion
  82.6 2.5 %multiply_bitcast_fusion = f32[16,256,128]{2,0,1:T(8,128)} fusion(f32[256,16,128]{2,1,0:T(8,128)S(1)} %gather_fusion, f32[256]{0:T(256)S(1)} %convert_element_type.43, pred[256]{0:T(512)(128)(4,1)S(1)} %compare_and_fusion), kind=kLoop, calls=%fused_computation.5 | loop fusion | flops 1048576 | bytes 4195584 | tf_op jit(solution)/shard_map/mul | solution.py:108
  85.2 8.3 %all-to-all-done.1 = f32[2,32,16,256]{3,2,0,1:T(8,128)} async-done(((f32[2,32,16,256]{3,2,0,1:T(8,128)}), f32[2,32,16,256]{3,2,0,1:T(8,128)}, u32[]{:S(2)}, u32[]{:S(2)}) %all-to-all-start.1) | async-done | bytes 1048608 | tf_op jit(solution)/shard_map/all_to_all | solution.py:149
  93.4 9.6 %all-to-all-start.2 = ((f32[16,256,128]{2,0,1:T(8,128)}), f32[16,256,128]{2,0,1:T(8,128)}, u32[]{:S(2)}, u32[]{:S(2)}) async-start(f32[16,256,128]{2,0,1:T(8,128)} %multiply_bitcast_fusion), calls=%async_computation.2 | async-start | bytes 4194304 | tf_op jit(solution)/shard_map/all_to_all | solution.py:109
  103.1 0.6 dynamic_slice.12
  103.7 0.7 compare_convert_fusion.1
  104.3 0.7 constant_dynamic-slice_fusion
  105.1 0.6 reduce-window.14
  106.0 0.7 compare_convert_fusion
  106.7 0.7 fusion.86
  107.9 1.9 copy.61
  109.8 0.5 reshape.154
  110.4 1.7 fusion.137
  112.1 40.2 %all-to-all-done.2 = f32[16,256,128]{2,0,1:T(8,128)} async-done(((f32[16,256,128]{2,0,1:T(8,128)}), f32[16,256,128]{2,0,1:T(8,128)}, u32[]{:S(2)}, u32[]{:S(2)}) %all-to-all-start.2) | async-done | bytes 2097184 | tf_op jit(solution)/shard_map/all_to_all | solution.py:109
  152.3 3.4 %fusion.4 = f32[16,128,128]{2,1,0:T(8,128)S(1)} fusion(f32[256,128,1]{0,1,2:T(8,128)S(1)} %convolution_bitcast_fusion, f32[16,256,128]{2,0,1:T(8,128)} %all-to-all-done.2), kind=kOutput, calls=%fused_computation.12 | convolution fusion | flops 805306368 | bytes 3276800 | tf_op jit(solution)/shard_map/lic,ib->lbc/dot_general | solution.py:127
  155.9 1.4 add.2442
  157.5 2.1 collective-permute-start.1
  159.6 1.3 collective-permute-start
  161.3 1.5 collective-permute-done
  162.9 0.7 fusion.13
  163.6 1.7 fusion.135
  165.4 5.2 %collective-permute-start.3 = (f32[17,1,1024]{2,1,0:T(1,128)S(1)}, f32[17,1,1024]{2,1,0:T(1,128)S(1)}, u32[]{:S(2)}, u32[]{:S(2)}) collective-permute-start(f32[17,1,1024]{2,1,0:T(1,128)S(1)} %get-tuple-element.88), channel_id=1, source_target_pairs={{0,16},{16,32},{32,48},{48,64},{64,80},{80,96},{96,112},{112,128},... | collective-permute-start | bytes 208904 | tf_op jit(solution)/shard_map/ppermute | solution.py:19
  170.7 1.5 collective-permute-start.2
  172.2 1.7 fusion.35
  173.9 2.1 %reduce_sum.39 = f32[8,16,1024]{2,1,0:T(8,128)} reduce(f32[2,8,16,1024]{3,2,1,0:T(8,128)} %bitcast.265, f32[]{:T(128)} %constant.48.clone.1), dimensions={0}, to_apply=%region_7.8 | reduce | flops 131072 | bytes 1572868 | tf_op jit(solution)/shard_map/reduce_sum | solution.py:159
  176.4 0.9 copy-done.3
  177.6 0.6 fusion.20
  178.4 3.0 %collective-permute-start.5 = (f32[17,1,1024]{2,1,0:T(1,128)S(1)}, f32[17,1,1024]{2,1,0:T(1,128)S(1)}, u32[]{:S(2)}, u32[]{:S(2)}) collective-permute-start(f32[17,1,1024]{2,1,0:T(1,128)S(1)} %get-tuple-element.86), channel_id=1, source_target_pairs={{0,16},{16,32},{32,48},{48,64},{64,80},{80,96},{96,112},{112,128},... | collective-permute-start | bytes 208904 | tf_op jit(solution)/shard_map/ppermute | solution.py:19
  181.8 1.3 collective-permute-start.4
  183.4 2.3 %collective-permute-done.4 = f32[17,1,1024]{2,1,0:T(1,128)S(1)} collective-permute-done((f32[17,1,1024]{2,1,0:T(1,128)S(1)}, f32[17,1,1024]{2,1,0:T(1,128)S(1)}, u32[]{:S(2)}, u32[]{:S(2)}) %collective-permute-start.4) | collective-permute-done | bytes 69664 | tf_op jit(solution)/shard_map/ppermute | solution.py:21
  185.7 1.6 fusion.27
  187.3 15.6 %reduce-scatter.2.cloned.1.call-done = f32[8,16,256]{2,1,0:T(8,128)} async-done(((f32[8,16,1024]{2,1,0:T(8,128)}), f32[8,16,256]{2,1,0:T(8,128)}) %reduce-scatter.2.cloned.1.call-update) | async-done | bytes 131088 | tf_op jit(solution)/shard_map/reduce_scatter | solution.py:158
  (118 shorter events, 5.8 us)
Async XLA Ops:
  23.9 5.9 %copy-start.2 = (f32[2,8,16,1024]{3,2,1,0:T(8,128)S(1)}, f32[2,8,16,1024]{3,2,1,0:T(8,128)}, u32[]{:S(2)}) copy-start(f32[2,8,16,1024]{3,2,1,0:T(8,128)} %param.11) | copy-start | bytes 3145732
  23.9 24.2 %all-to-all-start = ((f32[4,1,98304]{2,1,0:T(1,128)}), f32[4,1,98304]{2,1,0:T(1,128)S(1)}, u32[]{:S(2)}, u32[]{:S(2)}) async-start(f32[4,1,98304]{2,1,0:T(1,128)} %reshape.176), calls=%async_computation | async-start | bytes 3145728 | tf_op jit(solution)/shard_map/all_to_all | solution.py:147
  29.8 1.1 copy-start.10
  29.8 1.1 copy-start.12
  29.8 2.2 %copy-start.11 = (s32[16,256]{1,0:T(8,128)S(1)}, s32[16,256]{1,0:T(8,128)}, u32[]{:S(2)}) copy-start(s32[16,256]{1,0:T(8,128)} %param.19) | copy-start | bytes 49156
  48.1 1.2 copy-start.1
  75.9 17.5 %all-to-all-start.1 = ((f32[2,32,16,256]{3,2,0,1:T(8,128)}), f32[2,32,16,256]{3,2,0,1:T(8,128)}, u32[]{:S(2)}, u32[]{:S(2)}) async-start(f32[2,32,16,256]{3,2,0,1:T(8,128)} %copy.59), calls=%async_computation.1 | async-start | bytes 2097152 | tf_op jit(solution)/shard_map/all_to_all | solution.py:149
  85.2 20.7 %copy-start.8 = (f32[16,1024]{1,0:T(8,128)S(1)}, f32[16,1024]{1,0:T(8,128)}, u32[]{:S(2)}) copy-start(f32[16,1024]{1,0:T(8,128)} %param.16) | copy-start | bytes 196612
  85.2 20.8 %copy-start.9 = (f32[16,1024]{1,0:T(8,128)S(1)}, f32[16,1024]{1,0:T(8,128)}, u32[]{:S(2)}) copy-start(f32[16,1024]{1,0:T(8,128)} %param.14) | copy-start | bytes 196612
  93.4 58.9 %all-to-all-start.2 = ((f32[16,256,128]{2,0,1:T(8,128)}), f32[16,256,128]{2,0,1:T(8,128)}, u32[]{:S(2)}, u32[]{:S(2)}) async-start(f32[16,256,128]{2,0,1:T(8,128)} %multiply_bitcast_fusion), calls=%async_computation.2 | async-start | bytes 4194304 | tf_op jit(solution)/shard_map/all_to_all | solution.py:109
  103.0 99.9 %reduce-scatter.2.cloned.1.call-start = ((), (), s32[]{:S(2)}) async-start(), calls=%async_computation.4 | async-start | bytes 655360 | tf_op jit(solution)/shard_map/reduce_scatter | solution.py:158
  155.8 1.4 copy-start
  155.8 1.4 copy-start.7
  157.5 3.8 %collective-permute-start.1 = (f32[34,1,1024]{2,1,0:T(1,128)S(1)}, f32[34,1,1024]{2,1,0:T(1,128)S(1)}, u32[]{:S(2)}, u32[]{:S(2)}) collective-permute-start(f32[34,1,1024]{2,1,0:T(1,128)S(1)} %get-tuple-element.84), channel_id=1, source_target_pairs={{0,16},{16,32},{32,48},{48,64},{64,80},{80,96},{96,112},{112,128},... | collective-permute-start | bytes 417800 | tf_op jit(solution)/shard_map/ppermute | solution.py:19
  159.6 3.3 %collective-permute-start = (f32[34,1,1024]{2,1,0:T(1,128)S(1)}, f32[34,1,1024]{2,1,0:T(1,128)S(1)}, u32[]{:S(2)}, u32[]{:S(2)}) collective-permute-start(f32[34,1,1024]{2,1,0:T(1,128)S(1)} %get-tuple-element.83), channel_id=1, source_target_pairs={{16,0},{32,16},{48,32},{64,48},{80,64},{96,80},{112,96},{128,112},... | collective-permute-start | bytes 417800 | tf_op jit(solution)/shard_map/ppermute | solution.py:21
  163.6 8.6 %copy-start.6 = (f32[16,16,1023]{2,1,0:T(8,128)S(1)}, f32[16,16,1023]{2,1,0:T(8,128)}, u32[]{:S(2)}) copy-start(f32[16,16,1023]{2,1,0:T(8,128)} %get-tuple-element.96) | copy-start | bytes 3142660
  165.3 6.9 %copy-start.5 = (f32[16,16,1023]{2,1,0:T(8,128)S(1)}, f32[16,16,1023]{2,1,0:T(8,128)}, u32[]{:S(2)}) copy-start(f32[16,16,1023]{2,1,0:T(8,128)} %get-tuple-element.95) | copy-start | bytes 3142660
  165.4 10.7 %collective-permute-start.3 = (f32[17,1,1024]{2,1,0:T(1,128)S(1)}, f32[17,1,1024]{2,1,0:T(1,128)S(1)}, u32[]{:S(2)}, u32[]{:S(2)}) collective-permute-start(f32[17,1,1024]{2,1,0:T(1,128)S(1)} %get-tuple-element.88), channel_id=1, source_target_pairs={{0,16},{16,32},{32,48},{48,64},{64,80},{80,96},{96,112},{112,128},... | collective-permute-start | bytes 208904 | tf_op jit(solution)/shard_map/ppermute | solution.py:19
  170.7 5.7 %collective-permute-start.2 = (f32[17,1,1024]{2,1,0:T(1,128)S(1)}, f32[17,1,1024]{2,1,0:T(1,128)S(1)}, u32[]{:S(2)}, u32[]{:S(2)}) collective-permute-start(f32[17,1,1024]{2,1,0:T(1,128)S(1)} %get-tuple-element.87), channel_id=1, source_target_pairs={{16,0},{32,16},{48,32},{64,48},{80,64},{96,80},{112,96},{128,112},... | collective-permute-start | bytes 208904 | tf_op jit(solution)/shard_map/ppermute | solution.py:21
  176.1 1.2 copy-start.3
  176.1 1.5 copy-start.4
  178.4 4.7 %collective-permute-start.5 = (f32[17,1,1024]{2,1,0:T(1,128)S(1)}, f32[17,1,1024]{2,1,0:T(1,128)S(1)}, u32[]{:S(2)}, u32[]{:S(2)}) collective-permute-start(f32[17,1,1024]{2,1,0:T(1,128)S(1)} %get-tuple-element.86), channel_id=1, source_target_pairs={{0,16},{16,32},{32,48},{48,64},{64,80},{80,96},{96,112},{112,128},... | collective-permute-start | bytes 208904 | tf_op jit(solution)/shard_map/ppermute | solution.py:19
  181.8 3.9 %collective-permute-start.4 = (f32[17,1,1024]{2,1,0:T(1,128)S(1)}, f32[17,1,1024]{2,1,0:T(1,128)S(1)}, u32[]{:S(2)}, u32[]{:S(2)}) collective-permute-start(f32[17,1,1024]{2,1,0:T(1,128)S(1)} %get-tuple-element.85), channel_id=1, source_target_pairs={{16,0},{32,16},{48,32},{64,48},{80,64},{96,80},{112,96},{128,112},... | collective-permute-start | bytes 208904 | tf_op jit(solution)/shard_map/ppermute | solution.py:21
Sparse Core Ops, SparseCore 0:
  176.2 26.7 reduce-scatter.1
where the time goes:
time: 211 us; the launch traced here: 210 us
  waiting for transfers between devices  81.3 us (39%)
  local copies, waits for them, and re-layouts  49.5 us (23%)
  starting transfers between devices  35.7 us (17%)
  other arithmetic  24.7 us (12%)
  between operations  14.8 us (7%)
  matrix products  3.79 us (2%)
    all_to_all x1, waiting for transfers between devices, deliver(): lax.all_to_all(packed, 'tile', split_axis=1, concat_axis=1, tiled=True)  40.2 us
    unnamed x43, local copies, waits for them, and re-layouts  19.7 us
    reduce_scatter x1, waiting for transfers between devices, shards(): lax.psum_scatter(jnp.sum(parent_adjoint, axis=0), 'tag', scatter_dimensio...  15.6 us
    all_to_all x1, waiting for transfers between devices, shards(): lax.all_to_all(stacked, 'lev', split_axis=3, concat_axis=1, tiled=True)  13.4 us
    ppermute x3, starting transfers between devices, extended(): lax.ppermute(tail, axis, [(i, (i + 1) % count) for i in range(ends)])  10.3 us
    all_to_all x1, starting transfers between devices, deliver(): lax.all_to_all(packed, 'tile', split_axis=1, concat_axis=1, tiled=True)  9.61 us
    all_to_all x2, local copies, waits for them, and re-layouts, shards(): lax.all_to_all(stacked, 'lev', split_axis=3, concat_axis=1, tiled=True)  8.35 us
    all_to_all x1, waiting for transfers between devices, shards(): lax.all_to_all(column_result, 'lev', split_axis=1, concat_axis=3, tiled=T...  8.27 us
  transfers between devices with their start and end apart: 10, of which 6 were waited for; matrix products, arithmetic and copies ran while one was open for 12% of the time, Pallas kernels for 0%

commit v1 on v0

--- a/solution.py
+++ b/solution.py
@@ -144,7 +144,10 @@
     tag_count = parent_field.shape[0]
     forcing = deliver(parent_field, strip_tile, strip_block, strip_target, strip_count)
     stacked = jnp.concatenate([parent_field, parent_mixing[None]], axis=0)
-    columns = lax.all_to_all(stacked, "lev", split_axis=3, concat_axis=1, tiled=True)
+    columns = jnp.concatenate(
+        lax.all_to_all(jnp.stack(jnp.split(stacked, lax.axis_size("lev"), axis=3)), "lev", 0, 0),
+        axis=1,
+    )
     column_result = tridiagonal(columns[:tag_count], columns[tag_count])
     solved = lax.all_to_all(column_result, "lev", split_axis=1, concat_axis=3, tiled=True)
     parent_adjoint, nest_adjoint = advance(

time: 211 us -> 172 us (0.82)
  local copies, waits for them, and re-layouts: 49.5 us -> 15.5 us
  other arithmetic: 24.7 us -> 19.9 us
    unnamed x43 -> x39, local copies, waits for them, and re-layouts: 19.7 us -> 1.35 us
    all_to_all x2 -> x1, local copies, waits for them, and re-layouts: 8.35 us -> 0.12 us  [shards(): lax.all_to_all(jnp.stack(jnp.split(stacked, lax.axis_size('lev'), axis=3)...]
    concatenate x1 -> x0, local copies, waits for them, and re-layouts: 6.92 us -> none  [shards(): stacked = jnp.concatenate([parent_field, parent_mixing[None]], axis=0)]
    all_to_all x1 -> x0, other arithmetic: 6.16 us -> none  [shards(): lax.all_to_all(stacked, 'lev', split_axis=3, concat_axis=1, tiled=True)]
    another operation x5 -> x7, other arithmetic: 1.3 us -> 4.15 us  [the longest x2 2.85 us: shards(): jnp.stack(jnp.split(stacked, lax.axis_size('lev'), axis=3))]
  transfers between devices with their start and end apart: 10 -> 10, of which waited for: 6 -> 6; matrix products, arithmetic and copies ran while one was open for 12% -> 15% of each run, Pallas kernels for 0% -> 0%
where the time goes in v1:
time: 172 us; the launch traced here: 171 us
  waiting for transfers between devices  81.4 us (47%)
  starting transfers between devices  35.5 us (21%)
  other arithmetic  19.9 us (12%)
  local copies, waits for them, and re-layouts  15.5 us (9%)
  between operations  14.7 us (9%)
  matrix products  3.78 us (2%)
    all_to_all x1, waiting for transfers between devices, deliver(): lax.all_to_all(packed, 'tile', split_axis=1, concat_axis=1, tiled=True)  40.2 us
    reduce_scatter x1, waiting for transfers between devices, shards(): lax.psum_scatter(jnp.sum(parent_adjoint, axis=0), 'tag', scatter_dimensio...  15.6 us
    all_to_all x1, waiting for transfers between devices, shards(): lax.all_to_all(jnp.stack(jnp.split(stacked, lax.axis_size('lev'), axis=3)...  13.4 us
    ppermute x3, starting transfers between devices, extended(): lax.ppermute(tail, axis, [(i, (i + 1) % count) for i in range(ends)])  10.4 us
    all_to_all x1, starting transfers between devices, deliver(): lax.all_to_all(packed, 'tile', split_axis=1, concat_axis=1, tiled=True)  9.61 us
    all_to_all x1, waiting for transfers between devices, shards(): lax.all_to_all(column_result, 'lev', split_axis=1, concat_axis=3, tiled=T...  8.3 us
    all_to_all x1, starting transfers between devices, shards(): lax.all_to_all(jnp.stack(jnp.split(stacked, lax.axis_size('lev'), axis=3)...  5.93 us
    all_to_all x1, starting transfers between devices, shards(): lax.all_to_all(column_result, 'lev', split_axis=1, concat_axis=3, tiled=T...  5.67 us
  transfers between devices with their start and end apart: 10, of which 6 were waited for; matrix products, arithmetic and copies ran while one was open for 15% of the time, Pallas kernels for 0%

profile of v1, /device:TPU:2, one launch (start us, length us, event | category | flops | bytes accessed | tf_op | source)
XLA Modules:
  0.0 170.8 jit_solution(6059116242555972395)
XLA Ops:
  7.2 1.5 fusion.41
  8.7 1.3 pad_maximum_fusion.5
  10.0 5.9 %all-to-all-start = ((f32[4,3,8,16,256]{4,3,2,1,0:T(8,128)}), f32[4,3,8,16,256]{4,3,2,1,0:T(8,128)S(1)}, u32[]{:S(2)}, u32[]{:S(2)}) async-start(f32[4,3,8,16,256]{4,3,2,1,0:T(8,128)} %pad_maximum_fusion.5), calls=%async_computation | async-start | bytes 3145728 | tf_op jit(solution)/shard_map/all_to_all | solution.py:148
  16.0 1.1 reshape.164
  17.2 0.6 reduce-window.16
  18.1 0.6 select_reduce_fusion
  18.9 1.8 %copy.49 = f32[16,128,128]{2,0,1:T(8,128)S(1)} copy(f32[16,128,128]{2,1,0:T(8,128)} %reshape.164) | data formatting | bytes 2097152 | tf_op jit(solution)/shard_map/reshape | solution.py:107
  20.8 13.4 %all-to-all-done = f32[4,3,8,16,256]{4,3,2,1,0:T(8,128)S(1)} async-done(((f32[4,3,8,16,256]{4,3,2,1,0:T(8,128)}), f32[4,3,8,16,256]{4,3,2,1,0:T(8,128)S(1)}, u32[]{:S(2)}, u32[]{:S(2)}) %all-to-all-start) | async-done | bytes 1572896 | tf_op jit(solution)/shard_map/all_to_all | solution.py:148
  35.2 0.4 constant_dynamic-update-slice_fusion.31
  36.0 1.0 copy.43
  37.1 5.7 %all-to-all-start.1 = ((f32[2,32,16,256]{3,2,0,1:T(8,128)}), f32[2,32,16,256]{3,2,0,1:T(8,128)}, u32[]{:S(2)}, u32[]{:S(2)}) async-start(f32[2,32,16,256]{3,2,0,1:T(8,128)} %copy.43), calls=%async_computation.1 | async-start | bytes 2097152 | tf_op jit(solution)/shard_map/all_to_all | solution.py:152
  42.7 1.0 gather_fusion
  43.8 2.5 %multiply_bitcast_fusion = f32[16,256,128]{2,0,1:T(8,128)} fusion(f32[256,16,128]{2,1,0:T(8,128)S(1)} %gather_fusion, f32[256]{0:T(256)S(1)} %convert_element_type.43, pred[256]{0:T(512)(128)(4,1)S(1)} %compare_and_fusion), kind=kLoop, calls=%fused_computation.8 | loop fusion | flops 1048576 | bytes 4195584 | tf_op jit(solution)/shard_map/mul | solution.py:108
  46.3 8.3 %all-to-all-done.1 = f32[2,32,16,256]{3,2,0,1:T(8,128)} async-done(((f32[2,32,16,256]{3,2,0,1:T(8,128)}), f32[2,32,16,256]{3,2,0,1:T(8,128)}, u32[]{:S(2)}, u32[]{:S(2)}) %all-to-all-start.1) | async-done | bytes 1048608 | tf_op jit(solution)/shard_map/all_to_all | solution.py:152
  54.6 9.6 %all-to-all-start.2 = ((f32[16,256,128]{2,0,1:T(8,128)}), f32[16,256,128]{2,0,1:T(8,128)}, u32[]{:S(2)}, u32[]{:S(2)}) async-start(f32[16,256,128]{2,0,1:T(8,128)} %multiply_bitcast_fusion), calls=%async_computation.2 | async-start | bytes 4194304 | tf_op jit(solution)/shard_map/all_to_all | solution.py:109
  64.3 0.6 dynamic_slice.12
  64.8 0.7 compare_convert_fusion.1
  65.5 0.7 constant_dynamic-slice_fusion
  66.2 0.6 reduce-window.14
  67.2 0.7 fusion.93
  67.9 0.7 compare_convert_fusion
  68.6 0.4 convolution_bitcast_fusion
  69.0 1.9 %copy.45 = f32[2,8,16,4,256]{4,3,2,1,0:T(4,128)S(1)} copy(f32[2,8,16,4,256]{4,2,0,1,3:T(8,128)} %bitcast.105) | data formatting | bytes 2097152 | tf_op jit(solution)/shard_map/all_to_all | solution.py:152
  71.0 0.5 reshape.159
  71.5 1.7 fusion.144
  73.2 40.2 %all-to-all-done.2 = f32[16,256,128]{2,0,1:T(8,128)} async-done(((f32[16,256,128]{2,0,1:T(8,128)}), f32[16,256,128]{2,0,1:T(8,128)}, u32[]{:S(2)}, u32[]{:S(2)}) %all-to-all-start.2) | async-done | bytes 2097184 | tf_op jit(solution)/shard_map/all_to_all | solution.py:109
  113.4 3.4 %fusion.4 = f32[16,128,128]{2,1,0:T(8,128)S(1)} fusion(f32[256,128,1]{0,1,2:T(8,128)S(1)} %convolution_bitcast_fusion, f32[16,256,128]{2,0,1:T(8,128)} %all-to-all-done.2), kind=kOutput, calls=%fused_computation.19 | convolution fusion | flops 805306368 | bytes 3276800 | tf_op jit(solution)/shard_map/lic,ib->lbc/dot_general | solution.py:127
  117.0 1.4 add.2442
  118.7 2.1 %collective-permute-start.1 = (f32[34,1,1024]{2,1,0:T(1,128)S(1)}, f32[34,1,1024]{2,1,0:T(1,128)S(1)}, u32[]{:S(2)}, u32[]{:S(2)}) collective-permute-start(f32[34,1,1024]{2,1,0:T(1,128)S(1)} %get-tuple-element.84), channel_id=1, source_target_pairs={{0,16},{16,32},{32,48},{48,64},{64,80},{80,96},{96,112},{112,128},... | collective-permute-start | bytes 417800 | tf_op jit(solution)/shard_map/ppermute | solution.py:19
  120.8 1.3 collective-permute-start
  122.1 0.4 fusion.143
  122.5 1.5 collective-permute-done
  124.0 0.7 fusion.13
  124.9 1.7 fusion.142
  126.6 5.3 %collective-permute-start.3 = (f32[17,1,1024]{2,1,0:T(1,128)S(1)}, f32[17,1,1024]{2,1,0:T(1,128)S(1)}, u32[]{:S(2)}, u32[]{:S(2)}) collective-permute-start(f32[17,1,1024]{2,1,0:T(1,128)S(1)} %get-tuple-element.92), channel_id=1, source_target_pairs={{0,16},{16,32},{32,48},{48,64},{64,80},{80,96},{96,112},{112,128},... | collective-permute-start | bytes 208904 | tf_op jit(solution)/shard_map/ppermute | solution.py:19
  131.9 1.3 collective-permute-start.2
  133.2 1.7 %fusion.35 = f32[16,16,1024]{2,1,0:T(8,128)} fusion(f32[16,16,1024]{2,1,0:T(8,128)S(1)} %reshape.159, f32[34,1,1024]{2,1,0:T(1,128)S(1)} %collective-permute-done.1, f32[1,16,1024]{2,1,0:T(8,128)S(1)} %bitcast.259, f32[16,16,1024]{2,1,0:T(8,128)S(1)} %bitcast.236, f32[1,16,1024]{2,1,0:T(8,128)S(1)} %bitcast.275, f32[34,1,1024]{2,1,0:T(1,128)S(1)} %collective-permute-done, ...), kind=kLoop, calls=%fused_computation.61 | loop fusion | flops 5242880 | bytes 5912576 | tf_op jit(solution)/shard_map/add | solution.py:61
  134.9 2.1 %reduce_sum.39 = f32[8,16,1024]{2,1,0:T(8,128)} reduce(f32[2,8,16,1024]{3,2,1,0:T(8,128)} %bitcast.270, f32[]{:T(128)} %constant.48.clone.1), dimensions={0}, to_apply=%region_7.8 | reduce | flops 131072 | bytes 1572868 | tf_op jit(solution)/shard_map/reduce_sum | solution.py:162
  137.4 0.9 copy-done.2
  138.3 0.3 copy-done.3
  138.6 0.6 fusion.20
  139.3 3.0 %collective-permute-start.5 = (f32[17,1,1024]{2,1,0:T(1,128)S(1)}, f32[17,1,1024]{2,1,0:T(1,128)S(1)}, u32[]{:S(2)}, u32[]{:S(2)}) collective-permute-start(f32[17,1,1024]{2,1,0:T(1,128)S(1)} %get-tuple-element.90), channel_id=1, source_target_pairs={{0,16},{16,32},{32,48},{48,64},{64,80},{80,96},{96,112},{112,128},... | collective-permute-start | bytes 208904 | tf_op jit(solution)/shard_map/ppermute | solution.py:19
  142.4 0.4 fusion.141
  142.8 1.3 collective-permute-start.4
  144.1 0.3 fusion.3
  144.4 2.3 %collective-permute-done.4 = f32[17,1,1024]{2,1,0:T(1,128)S(1)} collective-permute-done((f32[17,1,1024]{2,1,0:T(1,128)S(1)}, f32[17,1,1024]{2,1,0:T(1,128)S(1)}, u32[]{:S(2)}, u32[]{:S(2)}) %collective-permute-start.4) | collective-permute-done | bytes 69664 | tf_op jit(solution)/shard_map/ppermute | solution.py:21
  146.7 1.6 fusion.27
  148.3 15.6 %reduce-scatter.2.cloned.1.call-done = f32[8,16,256]{2,1,0:T(8,128)} async-done(((f32[8,16,1024]{2,1,0:T(8,128)}), f32[8,16,256]{2,1,0:T(8,128)}) %reduce-scatter.2.cloned.1.call-update) | async-done | bytes 131088 | tf_op jit(solution)/shard_map/reduce_scatter | solution.py:161
  (110 shorter events, 3.3 us)
Async XLA Ops:
  10.0 5.9 %copy-start.1 = (f32[2,8,16,1024]{3,2,1,0:T(8,128)S(1)}, f32[2,8,16,1024]{3,2,1,0:T(8,128)}, u32[]{:S(2)}) copy-start(f32[2,8,16,1024]{3,2,1,0:T(8,128)} %param.11) | copy-start | bytes 3145732
  10.0 24.2 %all-to-all-start = ((f32[4,3,8,16,256]{4,3,2,1,0:T(8,128)}), f32[4,3,8,16,256]{4,3,2,1,0:T(8,128)S(1)}, u32[]{:S(2)}, u32[]{:S(2)}) async-start(f32[4,3,8,16,256]{4,3,2,1,0:T(8,128)} %pad_maximum_fusion.5), calls=%async_computation | async-start | bytes 3145728 | tf_op jit(solution)/shard_map/all_to_all | solution.py:148
  16.0 1.1 copy-start.9
  16.0 1.1 copy-start.11
  16.0 2.2 %copy-start.10 = (s32[16,256]{1,0:T(8,128)S(1)}, s32[16,256]{1,0:T(8,128)}, u32[]{:S(2)}) copy-start(s32[16,256]{1,0:T(8,128)} %param.19) | copy-start | bytes 49156
  37.1 17.5 %all-to-all-start.1 = ((f32[2,32,16,256]{3,2,0,1:T(8,128)}), f32[2,32,16,256]{3,2,0,1:T(8,128)}, u32[]{:S(2)}, u32[]{:S(2)}) async-start(f32[2,32,16,256]{3,2,0,1:T(8,128)} %copy.43), calls=%async_computation.1 | async-start | bytes 2097152 | tf_op jit(solution)/shard_map/all_to_all | solution.py:152
  46.3 20.8 %copy-start.8 = (f32[16,1024]{1,0:T(8,128)S(1)}, f32[16,1024]{1,0:T(8,128)}, u32[]{:S(2)}) copy-start(f32[16,1024]{1,0:T(8,128)} %param.14) | copy-start | bytes 196612
  46.3 20.8 %copy-start.7 = (f32[16,1024]{1,0:T(8,128)S(1)}, f32[16,1024]{1,0:T(8,128)}, u32[]{:S(2)}) copy-start(f32[16,1024]{1,0:T(8,128)} %param.16) | copy-start | bytes 196612
  54.6 58.9 %all-to-all-start.2 = ((f32[16,256,128]{2,0,1:T(8,128)}), f32[16,256,128]{2,0,1:T(8,128)}, u32[]{:S(2)}, u32[]{:S(2)}) async-start(f32[16,256,128]{2,0,1:T(8,128)} %multiply_bitcast_fusion), calls=%async_computation.2 | async-start | bytes 4194304 | tf_op jit(solution)/shard_map/all_to_all | solution.py:109
  64.2 99.7 %reduce-scatter.2.cloned.1.call-start = ((), (), s32[]{:S(2)}) async-start(), calls=%async_computation.4 | async-start | bytes 655360 | tf_op jit(solution)/shard_map/reduce_scatter | solution.py:161
  117.0 1.4 copy-start
  117.0 1.4 copy-start.6
  118.7 3.8 %collective-permute-start.1 = (f32[34,1,1024]{2,1,0:T(1,128)S(1)}, f32[34,1,1024]{2,1,0:T(1,128)S(1)}, u32[]{:S(2)}, u32[]{:S(2)}) collective-permute-start(f32[34,1,1024]{2,1,0:T(1,128)S(1)} %get-tuple-element.84), channel_id=1, source_target_pairs={{0,16},{16,32},{32,48},{48,64},{64,80},{80,96},{96,112},{112,128},... | collective-permute-start | bytes 417800 | tf_op jit(solution)/shard_map/ppermute | solution.py:19
  120.8 3.3 %collective-permute-start = (f32[34,1,1024]{2,1,0:T(1,128)S(1)}, f32[34,1,1024]{2,1,0:T(1,128)S(1)}, u32[]{:S(2)}, u32[]{:S(2)}) collective-permute-start(f32[34,1,1024]{2,1,0:T(1,128)S(1)} %get-tuple-element.83), channel_id=1, source_target_pairs={{16,0},{32,16},{48,32},{64,48},{80,64},{96,80},{112,96},{128,112},... | collective-permute-start | bytes 417800 | tf_op jit(solution)/shard_map/ppermute | solution.py:21
  124.9 8.3 %copy-start.4 = (f32[16,16,1023]{2,1,0:T(8,128)S(1)}, f32[16,16,1023]{2,1,0:T(8,128)}, u32[]{:S(2)}) copy-start(f32[16,16,1023]{2,1,0:T(8,128)} %get-tuple-element.99) | copy-start | bytes 3142660
  124.9 8.3 %copy-start.5 = (f32[16,16,1023]{2,1,0:T(8,128)S(1)}, f32[16,16,1023]{2,1,0:T(8,128)}, u32[]{:S(2)}) copy-start(f32[16,16,1023]{2,1,0:T(8,128)} %get-tuple-element.100) | copy-start | bytes 3142660
  126.6 10.5 %collective-permute-start.3 = (f32[17,1,1024]{2,1,0:T(1,128)S(1)}, f32[17,1,1024]{2,1,0:T(1,128)S(1)}, u32[]{:S(2)}, u32[]{:S(2)}) collective-permute-start(f32[17,1,1024]{2,1,0:T(1,128)S(1)} %get-tuple-element.92), channel_id=1, source_target_pairs={{0,16},{16,32},{32,48},{48,64},{64,80},{80,96},{96,112},{112,128},... | collective-permute-start | bytes 208904 | tf_op jit(solution)/shard_map/ppermute | solution.py:19
  131.9 5.5 %collective-permute-start.2 = (f32[17,1,1024]{2,1,0:T(1,128)S(1)}, f32[17,1,1024]{2,1,0:T(1,128)S(1)}, u32[]{:S(2)}, u32[]{:S(2)}) collective-permute-start(f32[17,1,1024]{2,1,0:T(1,128)S(1)} %get-tuple-element.91), channel_id=1, source_target_pairs={{16,0},{32,16},{48,32},{64,48},{80,64},{96,80},{112,96},{128,112},... | collective-permute-start | bytes 208904 | tf_op jit(solution)/shard_map/ppermute | solution.py:21
  137.0 1.2 copy-start.2
  137.1 1.5 copy-start.3
  139.3 4.7 %collective-permute-start.5 = (f32[17,1,1024]{2,1,0:T(1,128)S(1)}, f32[17,1,1024]{2,1,0:T(1,128)S(1)}, u32[]{:S(2)}, u32[]{:S(2)}) collective-permute-start(f32[17,1,1024]{2,1,0:T(1,128)S(1)} %get-tuple-element.90), channel_id=1, source_target_pairs={{0,16},{16,32},{32,48},{48,64},{64,80},{80,96},{96,112},{112,128},... | collective-permute-start | bytes 208904 | tf_op jit(solution)/shard_map/ppermute | solution.py:19
  142.8 3.9 %collective-permute-start.4 = (f32[17,1,1024]{2,1,0:T(1,128)S(1)}, f32[17,1,1024]{2,1,0:T(1,128)S(1)}, u32[]{:S(2)}, u32[]{:S(2)}) collective-permute-start(f32[17,1,1024]{2,1,0:T(1,128)S(1)} %get-tuple-element.89), channel_id=1, source_target_pairs={{16,0},{32,16},{48,32},{64,48},{80,64},{96,80},{112,96},{128,112},... | collective-permute-start | bytes 208904 | tf_op jit(solution)/shard_map/ppermute | solution.py:21
Sparse Core Ops, SparseCore 0:
  137.2 26.7 reduce-scatter.1
